TPU v7x, 128 devices: a whole 4x4x4 slice. The times are simulated.
128 devices in a mesh: src: 4 (over x), own: 32 (over y, z, core).
Axes of the slice: x: 4, y: 4, z: 4, core: 2. Of those that a mesh axis runs over, the one named last changes fastest.
Arguments:
- embeddings: bfloat16 [24576, 1024], P(('src', 'own'))
- cluster_ids: int32 [24576], P(('src', 'own')), may hold values from 0 to 1023, as said below
Outputs:
- best_similarity: float32 [24576], P(('src', 'own'))
Inputs may be any that keep to these rules, and one draw needn't show every extreme that they name: A document's owner shard is cluster_ids // 32. Among the rows of one device at most 12 have one owner shard, and in every draw one owner shard gets exactly 12 rows from every device.
All inputs are finite; a program needn't handle non-finite values.
Results may differ from a plain program's by a relative error of at most 0.00037.
Values may be sent and summed in bfloat16 or wider, within the bound.
A program may use at most 64 MiB of HBM per device.

v0:
```python
import math

import jax
import jax.numpy as jnp
from jax import lax
from jax.sharding import PartitionSpec as P

CL_OWN = 32


def normalize_rows(embeddings):
    values = embeddings.astype(jnp.float32)
    scale = lax.rsqrt(jnp.mean(values * values, axis=1, keepdims=True) + 1e-06) / math.sqrt(
        values.shape[1]
    )
    return (values * scale).astype(jnp.bfloat16)


def block_best(running, own_rows, own_meta, other_rows, other_meta):
    scores = jnp.dot(own_rows, other_rows.T, preferred_element_type=jnp.float32)
    same_group = (own_meta[:, 0:1] == other_meta[None, :, 0]) & (
        own_meta[:, 1:2] != other_meta[None, :, 1]
    )
    found = jnp.max(jnp.where(same_group, scores, jnp.float32(-1.0)), axis=1)
    return jnp.maximum(running, found)


def scan_blocks(running, own_rows, own_meta, other_rows, other_meta, block_rows):
    width = other_rows.shape[1]
    stacked_rows = other_rows.reshape(-1, block_rows, width)
    stacked_meta = other_meta.reshape(-1, block_rows, 2)

    def one_block(current, pieces):
        return (block_best(current, own_rows, own_meta, pieces[0], pieces[1]), 0)

    result, unused = lax.scan(one_block, running, (stacked_rows, stacked_meta))
    return result


def shards(embeddings, cluster_ids):
    rows_here = embeddings.shape[0]
    owners = lax.axis_size("own")
    sources = lax.axis_size("src")
    capacity = 2 * rows_here // owners
    slab_rows = owners * capacity
    unit = normalize_rows(embeddings)
    first_row = (lax.axis_index("src") * owners + lax.axis_index("own")) * rows_here
    positions = first_row + jnp.arange(rows_here, dtype=jnp.int32)
    owner_of = cluster_ids // CL_OWN
    onehot = (owner_of[:, None] == jnp.arange(owners, dtype=jnp.int32)[None, :]).astype(jnp.int32)
    slot_rank = jnp.sum(jnp.cumsum(onehot, axis=0) * onehot, axis=1) - 1
    slot_index = owner_of * capacity + slot_rank
    send_rows = jnp.zeros((slab_rows, unit.shape[1]), jnp.bfloat16).at[slot_index].set(unit)
    send_meta = (
        jnp.full((slab_rows, 2), -1, jnp.int32)
        .at[slot_index]
        .set(jnp.stack([cluster_ids, positions], axis=1))
    )
    initial = jnp.full((slab_rows,), -1.0, jnp.float32)
    every_rows = jnp.tile(send_rows, (sources, 1))
    every_meta = jnp.tile(send_meta, (sources, 1))
    got_rows, got_meta = (
        lax.all_to_all(every_rows, ("src", "own"), split_axis=0, concat_axis=0, tiled=True),
        lax.all_to_all(every_meta, ("src", "own"), split_axis=0, concat_axis=0, tiled=True),
    )
    src_index = lax.axis_index("src")
    own_rows = lax.dynamic_slice_in_dim(got_rows, src_index * slab_rows, slab_rows, 0)
    own_meta = lax.dynamic_slice_in_dim(got_meta, src_index * slab_rows, slab_rows, 0)
    best = scan_blocks(initial, own_rows, own_meta, got_rows, got_meta, slab_rows)
    returned = lax.all_to_all(best, "own", split_axis=0, concat_axis=0, tiled=True)
    return returned[slot_index]


def solution(mesh):
    in_specs = (P(("src", "own"), None), P(("src", "own")))
    out_specs = P(("src", "own"))
    return jax.shard_map(shards, mesh=mesh, in_specs=in_specs, out_specs=out_specs, check_vma=False)
```

profile of v0, /device:TPU:1, one launch (start us, length us, event | category | flops | bytes accessed | tf_op | source)
XLA Modules:
  0.0 121.7 jit_solution(6402041084793041459)
XLA Ops:
  0.0 0.7 and_select_fusion
  0.7 0.6 reduce-window.6
  1.3 0.2 slice_reduce_fusion.4
  1.5 0.1 bitcast_bitcast_fusion
  1.7 0.7 compare_select_fusion
  2.4 0.7 pad_add_fusion
  3.0 0.1 copy.14
  3.2 1.1 scatter_custom_fusion
  4.2 0.1 copy.15
  4.3 0.2 all_to_all.24
  4.5 0.8 copy.16
  5.3 11.5 %all-to-all-start = ((s32[128,12,2]{1,2,0:T(2,128)}), s32[128,12,2]{1,2,0:T(2,128)S(1)}, u32[]{:S(2)}, u32[]{:S(2)}) async-start(s32[128,12,2]{1,2,0:T(2,128)} %copy.16), calls=%async_computation | async-start | bytes 262144 | tf_op jit(solution)/shard_map/all_to_all | solution.py:64
  16.8 1.2 fusion.5
  17.9 2.9 %scatter_custom_fusion.1 = bf16[384,1024]{1,0:T(8,128)(2,1)} fusion(s32[192]{0:T(256)S(1)} %compare_select_fusion, bf16[192,1024]{1,0:T(8,128)(2,1)} %param.4, f32[192]{0:T(256)S(1)} %rsqrt_multiply_fusion, bf16[]{:T(256)} %constant.35.clone.1), kind=kCustom, calls=%fused_computation.20 | custom fusion | flops 589824 | bytes 1180674 | tf_op jit(solution)/shard_map/scatter | solution.py:53
  20.8 1.5 %tile.5 = bf16[4,384,1024]{2,1,0:T(8,128)(2,1)S(1)} broadcast(bf16[384,1024]{1,0:T(8,128)(2,1)} %scatter_custom_fusion.1), dimensions={1,2} | broadcast | bytes 3932160 | tf_op jit(solution)/shard_map/tile | solution.py:60
  22.4 2.7 %all_to_all.27 = bf16[128,12,1024]{2,1,0:T(8,128)(2,1)} reshape(bf16[4,384,1024]{2,1,0:T(8,128)(2,1)S(1)} %tile.5) | data formatting | bytes 6291456 | tf_op jit(solution)/shard_map/all_to_all | solution.py:63
  25.0 1.5 %all-to-all-done = s32[128,12,2]{1,2,0:T(2,128)S(1)} async-done(((s32[128,12,2]{1,2,0:T(2,128)}), s32[128,12,2]{1,2,0:T(2,128)S(1)}, u32[]{:S(2)}, u32[]{:S(2)}) %all-to-all-start) | async-done | bytes 12320 | tf_op jit(solution)/shard_map/all_to_all | solution.py:64
  26.5 8.7 %all-to-all-start.1 = ((bf16[128,12,1024]{2,1,0:T(8,128)(2,1)}), bf16[128,12,1024]{2,1,0:T(8,128)(2,1)}, u32[]{:S(2)}, u32[]{:S(2)}) async-start(bf16[128,12,1024]{2,1,0:T(8,128)(2,1)} %all_to_all.27), calls=%async_computation.1 | async-start | bytes 8388608 | tf_op jit(solution)/shard_map/all_to_all | solution.py:63
  35.3 0.1 reshape.57
  35.4 0.1 all_to_all.26
  35.6 52.5 %all-to-all-done.1 = bf16[128,12,1024]{2,1,0:T(8,128)(2,1)} async-done(((bf16[128,12,1024]{2,1,0:T(8,128)(2,1)}), bf16[128,12,1024]{2,1,0:T(8,128)(2,1)}, u32[]{:S(2)}, u32[]{:S(2)}) %all-to-all-start.1) | async-done | bytes 3145760 | tf_op jit(solution)/shard_map/all_to_all | solution.py:63
  88.0 4.7 %all_to_all.29 = bf16[1536,1024]{1,0:T(8,128)(2,1)S(1)} reshape(bf16[128,12,1024]{2,1,0:T(8,128)(2,1)} %all-to-all-done.1) | data formatting | bytes 6291456 | tf_op jit(solution)/shard_map/all_to_all | solution.py:63
  92.8 0.9 constant_dynamic-slice_fusion.1
  93.7 4.7 %reshape.58 = bf16[4,384,1024]{2,1,0:T(8,128)(2,1)S(1)} reshape(bf16[128,12,1024]{2,1,0:T(8,128)(2,1)} %all-to-all-done.1) | data formatting | bytes 6291456 | tf_op jit(solution)/shard_map/reshape | solution.py:30
  98.4 7.4 %while.11 = (s32[]{:T(128)}, f32[384]{0:T(512)S(1)}, s32[384,2]{0,1:T(2,128)S(1)}, s32[4,384,2]{1,0,2:T(4,128)S(1)}, bf16[4,384,1024]{2,1,0:T(8,128)(2,1)S(1)}, ...) while((s32[]{:T(128)}, f32[384]{0:T(512)S(1)}, s32[384,2]{0,1:T(2,128)S(1)}, ...), condition=%wide.region_8.9_spmd.clone, body=%wide.region_6.8_spmd.clone.sunk | while | flops 302727552 | bytes 1611887 | solution.py:36
  98.5 1.7 %fusion.20 = f32[384]{0:T(512)S(1)} fusion(bf16[384,1024]{1,0:T(8,128)(2,1)} %get-tuple-element.161, bf16[4,384,1024]{2,1,0:T(8,128)(2,1)S(1)} %get-tuple-element.160, s32[]{:T(128)S(6)} %copy.32, s32[384]{0:T(512)S(1)} %get-tuple-element.136, s32[384]{0:T(512)S(1)} %get-tuple-element.137, s32[384]{0:T(512)S(1)} %get-tuple-element.138, ...), kind=kOutput, calls=%fused_computation.5.clone.1 | convolution fusion | flops 302726784 | bytes 1582596 | tf_op jit(solution)/shard_map/while/body/eval_jaxpr/dot_general | solution.py:20
  100.4 1.7 %fusion.20 = f32[384]{0:T(512)S(1)} fusion(bf16[384,1024]{1,0:T(8,128)(2,1)} %get-tuple-element.161, bf16[4,384,1024]{2,1,0:T(8,128)(2,1)S(1)} %get-tuple-element.160, s32[]{:T(128)S(6)} %copy.32, s32[384]{0:T(512)S(1)} %get-tuple-element.136, s32[384]{0:T(512)S(1)} %get-tuple-element.137, s32[384]{0:T(512)S(1)} %get-tuple-element.138, ...), kind=kOutput, calls=%fused_computation.5.clone.1 | convolution fusion | flops 302726784 | bytes 1582596 | tf_op jit(solution)/shard_map/while/body/eval_jaxpr/dot_general | solution.py:20
  102.2 1.7 %fusion.20 = f32[384]{0:T(512)S(1)} fusion(bf16[384,1024]{1,0:T(8,128)(2,1)} %get-tuple-element.161, bf16[4,384,1024]{2,1,0:T(8,128)(2,1)S(1)} %get-tuple-element.160, s32[]{:T(128)S(6)} %copy.32, s32[384]{0:T(512)S(1)} %get-tuple-element.136, s32[384]{0:T(512)S(1)} %get-tuple-element.137, s32[384]{0:T(512)S(1)} %get-tuple-element.138, ...), kind=kOutput, calls=%fused_computation.5.clone.1 | convolution fusion | flops 302726784 | bytes 1582596 | tf_op jit(solution)/shard_map/while/body/eval_jaxpr/dot_general | solution.py:20
  104.0 1.7 %fusion.20 = f32[384]{0:T(512)S(1)} fusion(bf16[384,1024]{1,0:T(8,128)(2,1)} %get-tuple-element.161, bf16[4,384,1024]{2,1,0:T(8,128)(2,1)S(1)} %get-tuple-element.160, s32[]{:T(128)S(6)} %copy.32, s32[384]{0:T(512)S(1)} %get-tuple-element.136, s32[384]{0:T(512)S(1)} %get-tuple-element.137, s32[384]{0:T(512)S(1)} %get-tuple-element.138, ...), kind=kOutput, calls=%fused_computation.5.clone.1 | convolution fusion | flops 302726784 | bytes 1582596 | tf_op jit(solution)/shard_map/while/body/eval_jaxpr/dot_general | solution.py:20
  105.8 0.7 all_to_all.30
  106.5 4.6 %all-to-all-start.2 = ((f32[32,12,1]{1,2,0:T(1,128)}), f32[32,12,1]{1,2,0:T(1,128)S(1)}, u32[]{:S(2)}, u32[]{:S(2)}) async-start(f32[32,12,1]{1,2,0:T(1,128)} %bitcast.2), calls=%async_computation.2 | async-start | bytes 32768 | tf_op jit(solution)/shard_map/all_to_all | solution.py:70
  111.2 7.0 %all-to-all-done.2 = f32[32,12,1]{1,2,0:T(1,128)S(1)} async-done(((f32[32,12,1]{1,2,0:T(1,128)}), f32[32,12,1]{1,2,0:T(1,128)S(1)}, u32[]{:S(2)}, u32[]{:S(2)}) %all-to-all-start.2) | async-done | bytes 1568 | tf_op jit(solution)/shard_map/all_to_all | solution.py:70
  118.2 0.5 broadcast.86
  118.7 0.7 reduce.13
  119.4 0.1 all_to_all.32
  119.5 2.2 %gather_fusion = f32[192]{0:T(256)} fusion(f32[384]{0:T(512)S(1)} %all_to_all.32, s32[1024]{0:T(1024)S(1)} %pad_clamp_fusion), kind=kCustom, calls=%fused_computation | custom fusion | bytes 2304 | tf_op jit(solution)/shard_map/gather | solution.py:71
  (28 shorter events, 0.4 us)
Async XLA Ops:
  5.3 21.2 %all-to-all-start = ((s32[128,12,2]{1,2,0:T(2,128)}), s32[128,12,2]{1,2,0:T(2,128)S(1)}, u32[]{:S(2)}, u32[]{:S(2)}) async-start(s32[128,12,2]{1,2,0:T(2,128)} %copy.16), calls=%async_computation | async-start | bytes 262144 | tf_op jit(solution)/shard_map/all_to_all | solution.py:64
  26.5 61.5 %all-to-all-start.1 = ((bf16[128,12,1024]{2,1,0:T(8,128)(2,1)}), bf16[128,12,1024]{2,1,0:T(8,128)(2,1)}, u32[]{:S(2)}, u32[]{:S(2)}) async-start(bf16[128,12,1024]{2,1,0:T(8,128)(2,1)} %all_to_all.27), calls=%async_computation.1 | async-start | bytes 8388608 | tf_op jit(solution)/shard_map/all_to_all | solution.py:63
  106.5 11.7 %all-to-all-start.2 = ((f32[32,12,1]{1,2,0:T(1,128)}), f32[32,12,1]{1,2,0:T(1,128)S(1)}, u32[]{:S(2)}, u32[]{:S(2)}) async-start(f32[32,12,1]{1,2,0:T(1,128)} %bitcast.2), calls=%async_computation.2 | async-start | bytes 32768 | tf_op jit(solution)/shard_map/all_to_all | solution.py:70
where the time goes:
time: 122 us
  waiting for transfers between devices  61 us (50%)
  starting transfers between devices  24.9 us (20%)
  local copies, waits for them, and re-layouts  20.9 us (17%)
  other arithmetic  7.61 us (6%)
  matrix products  6.98 us (6%)
    all_to_all x1, waiting for transfers between devices, shards(): lax.all_to_all(every_rows, ('src', 'own'), split_axis=0, concat_axis=0, t...  52.5 us
    all_to_all x1, starting transfers between devices, shards(): lax.all_to_all(every_meta, ('src', 'own'), split_axis=0, concat_axis=0, t...  11.5 us
    all_to_all x1, starting transfers between devices, shards(): lax.all_to_all(every_rows, ('src', 'own'), split_axis=0, concat_axis=0, t...  8.74 us
    all_to_all x2, local copies, waits for them, and re-layouts, shards(): lax.all_to_all(every_rows, ('src', 'own'), split_axis=0, concat_axis=0, t...  7.4 us
    all_to_all x1, waiting for transfers between devices, shards(): lax.all_to_all(best, 'own', split_axis=0, concat_axis=0, tiled=True)  7.04 us
    dot_general x4, matrix products, block_best(): scores = jnp.dot(own_rows, other_rows.T, preferred_element_type=jnp.float32)  6.98 us
    reshape x1, local copies, waits for them, and re-layouts, scan_blocks(): stacked_rows = other_rows.reshape(-1, block_rows, width)  4.71 us
    all_to_all x1, starting transfers between devices, shards(): lax.all_to_all(best, 'own', split_axis=0, concat_axis=0, tiled=True)  4.62 us
  transfers between devices with their start and end apart: 3, of which 3 were waited for; matrix products, arithmetic and copies ran while one was open for 5% of the time, Pallas kernels for 0%

commit v1 on v0

v1 whole, which is shorter than its diff:
```python
import functools
import math

import jax
import jax.numpy as jnp
from jax import lax
from jax.experimental import pallas as pl
from jax.experimental.pallas import tpu as pltpu
from jax.sharding import PartitionSpec as P

MESH = pl.DeviceIdType.MESH
F32, BF16, I32 = jnp.float32, jnp.bfloat16, jnp.int32

D = 1024
ROWS = 192
CAP = 12
OWNERS = 32
DEVS = 128
CL_OWN = 32
QUARTERS = 4
QW = D // QUARTERS
BLK = QUARTERS * CAP
GRP = 16
NGRP = DEVS // GRP
GROWS = GRP * CAP
RETW = 256


def home_of(owner):
    y, z, c = owner // 8, lax.rem(owner // 2, 4), lax.rem(owner, 2)
    return lax.rem(y + z + 2 * c, 4), owner


def shard_at(src, own):
    y, z, c = own // 8, lax.rem(own // 2, 4), lax.rem(own, 2)
    return lax.rem(y + z + 2 * c, 4) == src, own


def slot_of(src, own):
    y, z, c = own // 8, lax.rem(own // 2, 4), lax.rem(own, 2)
    return z * 32 + y * 8 + src * 2 + c


def device_at(slot):
    z, y, x, c = slot // 32, lax.rem(slot // 8, 4), lax.rem(slot // 2, 4), lax.rem(slot, 2)
    return x, y * 8 + z * 2 + c


def div12(v):
    return (v * 5462) >> 16


def dot_nn(a, b):
    return lax.dot_general(a, b, (((1,), (0,)), ((), ())), preferred_element_type=F32)


def dot_nt(a, b):
    return lax.dot_general(a, b, (((1,), (1,)), ((), ())), preferred_element_type=F32)


def dot_tn(a, b):
    return lax.dot_general(a, b, (((0,), (0,)), ((), ())), preferred_element_type=F32)


def iota(shape, dim):
    return lax.broadcasted_iota(I32, shape, dim)


def swap_matrix():
    i, j = iota((GROWS, GROWS), 0), iota((GROWS, GROWS), 1)
    ab = div12(i)
    a, b = ab >> 2, ab & 3
    return (j == b * BLK + a * CAP + (i - ab * CAP)).astype(BF16)


def kernel(
    emb_ref, ids_ref, out_ref,
    send, meta_send, recv, meta_recv, rows, id_col, id_row, best, back,
    send_sem, meta_send_sem, recv_sem, meta_recv_sem, back_send_sem, back_sem,
):
    src, own = lax.axis_index("src"), lax.axis_index("own")
    is_home, shard = shard_at(src, own)
    slot = slot_of(src, own)

    barrier = pltpu.get_barrier_semaphore()

    @pl.when(is_home)
    def _():
        def greet(i, carry):
            s, o = device_at(lax.rem(slot + i, DEVS))
            pl.semaphore_signal(barrier, inc=1, device_id=(s, o), device_id_type=MESH)
            return carry

        lax.fori_loop(1, DEVS, greet, 0)

    ids = ids_ref[...]
    owner = ids >> 5
    onehot = iota((OWNERS, ROWS), 0) == owner
    onehot_b = onehot.astype(BF16)
    upto = (iota((ROWS, ROWS), 0) <= iota((ROWS, ROWS), 1)).astype(BF16)
    counts = dot_nn(onehot_b, upto)
    rank = jnp.sum(jnp.where(onehot, counts, 0.0), axis=0, keepdims=True).astype(I32) - 1
    place = owner * CAP + rank
    pick = (iota((OWNERS * CAP, ROWS), 0) == place).astype(BF16)

    local = (ids - owner * CL_OWN + 1).astype(F32)
    by_rank = jnp.where(iota((128, ROWS), 0) == rank, local, 0.0).astype(BF16)
    meta_send[...] = (dot_nt(onehot_b, by_rank) - 1.0).reshape(OWNERS, 1, 128)

    values = emb_ref[...].astype(F32)
    mean = jnp.sum(values * values, axis=1, keepdims=True) * (1.0 / D)
    scale = lax.rsqrt(mean + 1e-06) * (1.0 / math.sqrt(D))
    unit = (values * scale).astype(BF16)
    packed = dot_nn(pick, unit).astype(BF16)
    swap = swap_matrix()
    for k in range(OWNERS // 4):
        part = packed[k * BLK : (k + 1) * BLK]
        stacked = jnp.concatenate([part[:, q * QW : (q + 1) * QW] for q in range(QUARTERS)], axis=0)
        send[pl.ds(4 * k, 4)] = dot_nn(swap, stacked).astype(BF16).reshape(4, BLK, QW)

    @pl.when(is_home)
    def _():
        pl.semaphore_wait(barrier, OWNERS - 1)

    @pl.when(jnp.logical_not(is_home))
    def _():
        pl.semaphore_wait(barrier, OWNERS)

    group = slot // GRP

    def give(i, carry):
        to = lax.rem(own + i, OWNERS)
        s, o = home_of(to)
        here = (s == src) & (o == own)

        @pl.when(jnp.logical_not(here))
        def _():
            pltpu.make_async_remote_copy(
                meta_send.at[to], meta_recv.at[slot], meta_send_sem, meta_recv_sem.at[group],
                device_id=(s, o), device_id_type=MESH,
            ).start()
            pltpu.make_async_remote_copy(
                send.at[to], recv.at[slot], send_sem, recv_sem.at[group],
                device_id=(s, o), device_id_type=MESH,
            ).start()

        @pl.when(here)
        def _():
            pltpu.make_async_copy(meta_send.at[to], meta_recv.at[slot], meta_recv_sem.at[group]).start()
            pltpu.make_async_copy(send.at[to], recv.at[slot], recv_sem.at[group]).start()

        return carry

    lax.fori_loop(0, OWNERS, give, 0)

    @pl.when(is_home)
    def _():
        lane_of = iota((GRP, GROWS), 1)
        spread = (div12(lane_of) == iota((GRP, GROWS), 0)).astype(BF16)
        nth_row = iota((GRP, GROWS), 0) == lane_of - div12(lane_of) * CAP
        sub = iota((GROWS, 128), 0)
        nth_col = iota((GROWS, 128), 1) == sub - div12(sub) * CAP
        not_self = iota((GROWS, GROWS), 0) != iota((GROWS, GROWS), 1)
        best[...] = jnp.full(best.shape, -1.0, F32)

        def one_group(g, carry):
            first = pl.multiple_of(g * GRP, GRP)
            block = meta_recv.at[pl.ds(first, GRP)]
            pltpu.make_async_copy(block, block, meta_recv_sem.at[g]).wait()
            block = recv.at[pl.ds(first, GRP)]
            pltpu.make_async_copy(block, block, recv_sem.at[g]).wait()
            ids_g = meta_recv[pl.ds(first, GRP)].reshape(GRP, 128).astype(BF16)
            wide = dot_tn(spread, ids_g)
            col_g = jnp.sum(jnp.where(nth_col, wide, 0.0), axis=1, keepdims=True)
            wide = dot_tn(ids_g, spread)[:GRP]
            row_g = jnp.sum(jnp.where(nth_row, wide, 0.0), axis=0, keepdims=True)
            id_col[g] = col_g
            id_row[g] = row_g
            for k in range(GRP // 4):
                four = recv[pl.ds(first + 4 * k, 4)].reshape(GROWS, QW)
                turned = dot_nn(swap, four).astype(BF16)
                at = pl.ds(pl.multiple_of(g * GROWS + k * BLK, 16), BLK)
                for q in range(QUARTERS):
                    rows[at, q * QW : (q + 1) * QW] = turned[q * BLK : (q + 1) * BLK]
            mine = rows[pl.ds(pl.multiple_of(g * GROWS, 16), GROWS), :]
            scores = dot_nt(mine, mine)
            keep = (col_g == row_g) & not_self
            found = jnp.max(jnp.where(keep, scores, -1.0), axis=0, keepdims=True)

            def earlier(h, found):
                other = rows[pl.ds(pl.multiple_of(h * GROWS, 16), GROWS), :]
                scores = dot_nt(other, mine)
                top = jnp.max(jnp.where(id_col[h] == row_g, scores, -1.0), axis=0, keepdims=True)
                scores = dot_nt(mine, other)
                top_h = jnp.max(jnp.where(col_g == id_row[h], scores, -1.0), axis=0, keepdims=True)
                best[h, :, :GROWS] = jnp.maximum(best[h, :, :GROWS], top_h)
                return jnp.maximum(found, top)

            found = lax.fori_loop(0, g, earlier, found)
            best[g, :, :GROWS] = jnp.maximum(found, -1.0)
            return carry

        lax.fori_loop(0, NGRP, one_group, 0)

        def give_back(i, carry):
            to = lax.rem(slot + i, DEVS)
            pltpu.make_async_remote_copy(
                best.at[to // GRP], back.at[shard], back_send_sem, back_sem,
                device_id=device_at(to), device_id_type=MESH,
            ).start()
            return carry

        lax.fori_loop(1, DEVS, give_back, 0)
        pltpu.make_async_copy(best.at[group], back.at[shard], back_sem).start()

    pltpu.make_async_copy(back, back, back_sem).wait()
    got = back[...].reshape(OWNERS, RETW)
    high = got.astype(BF16)
    rest = got - high.astype(F32)
    mid = rest.astype(BF16)
    low = (rest - mid.astype(F32)).astype(BF16)
    wide = dot_tn(high, onehot_b) + dot_tn(mid, onehot_b) + dot_tn(low, onehot_b)
    lane = lax.rem(slot, GRP) * CAP + rank
    out_ref[...] = jnp.sum(jnp.where(iota((RETW, ROWS), 0) == lane, wide, 0.0), axis=0, keepdims=True)

    @pl.when(is_home)
    def _():
        pltpu.make_async_copy(send.at[pl.ds(0, OWNERS - 1)], send.at[pl.ds(0, OWNERS - 1)], send_sem).wait()
        part = meta_send.at[pl.ds(0, OWNERS - 1)]
        pltpu.make_async_copy(part, part, meta_send_sem).wait()

        def sent(i, carry):
            pltpu.make_async_copy(best.at[0], best.at[0], back_send_sem).wait()
            return carry

        lax.fori_loop(1, DEVS, sent, 0)

    @pl.when(jnp.logical_not(is_home))
    def _():
        pltpu.make_async_copy(send, send, send_sem).wait()
        pltpu.make_async_copy(meta_send, meta_send, meta_send_sem).wait()


def shards(embeddings, cluster_ids):
    dma = pltpu.SemaphoreType.DMA
    out = pl.pallas_call(
        kernel,
        out_shape=jax.ShapeDtypeStruct((1, ROWS), F32),
        in_specs=[pl.BlockSpec(memory_space=pltpu.VMEM)] * 2,
        out_specs=pl.BlockSpec(memory_space=pltpu.VMEM),
        scratch_shapes=[
            pltpu.VMEM((OWNERS, BLK, QW), BF16),
            pltpu.VMEM((OWNERS, 1, 128), F32),
            pltpu.VMEM((DEVS, BLK, QW), BF16),
            pltpu.VMEM((DEVS, 1, 128), F32),
            pltpu.VMEM((DEVS * CAP, D), BF16),
            pltpu.VMEM((NGRP, GROWS, 1), F32),
            pltpu.VMEM((NGRP, 1, GROWS), F32),
            pltpu.VMEM((NGRP, 1, RETW), F32),
            pltpu.VMEM((OWNERS, 1, RETW), F32),
            dma, dma, dma((NGRP,)), dma((NGRP,)), dma, dma,
        ],
        compiler_params=pltpu.CompilerParams(
            collective_id=0, has_side_effects=True, vmem_limit_bytes=40 << 20
        ),
    )(embeddings, cluster_ids.reshape(1, ROWS))
    return out.reshape(ROWS)


def solution(mesh):
    in_specs = (P(("src", "own"), None), P(("src", "own")))
    out_specs = P(("src", "own"))
    return jax.shard_map(shards, mesh=mesh, in_specs=in_specs, out_specs=out_specs, check_vma=False)
```

time: 122 us -> 56.1 us (0.46)
  waiting for transfers between devices: 61 us -> 0 us
  Pallas kernels: 0 us -> 53.6 us
  starting transfers between devices: 24.9 us -> 0 us
  local copies, waits for them, and re-layouts: 20.9 us -> 2.24 us
  other arithmetic: 7.61 us -> 0 us
  matrix products: 6.98 us -> 0 us
    all_to_all x3 -> x0, waiting for transfers between devices: 61 us -> none  [the longest x1 52.5 us: shards(): lax.all_to_all(every_rows, ('src', 'own'), split_axis=0, concat_axis=0, t...]
    pallas_call x0 -> x1, Pallas kernels: none -> 53.6 us  [shards(): pl.pallas_call(kernel, out_shape=jax.ShapeDtypeStruct((1, ROWS), F32), in...]
    all_to_all x3 -> x0, starting transfers between devices: 24.9 us -> none  [the longest x1 11.5 us: shards(): lax.all_to_all(every_meta, ('src', 'own'), split_axis=0, concat_axis=0, t...]
    all_to_all x9 -> x0, local copies, waits for them, and re-layouts: 9.78 us -> none  [the longest x2 7.4 us: shards(): lax.all_to_all(every_rows, ('src', 'own'), split_axis=0, concat_axis=0, t...]
    dot_general x4 -> x0, matrix products: 6.98 us -> none  [block_best(): scores = jnp.dot(own_rows, other_rows.T, preferred_element_type=jnp.float32)]
    reshape x2 -> x0, local copies, waits for them, and re-layouts: 4.84 us -> none  [the longest x1 4.71 us: scan_blocks(): stacked_rows = other_rows.reshape(-1, block_rows, width)]
    scatter x1 -> x0, other arithmetic: 2.87 us -> none  [shards(): jnp.zeros((slab_rows, unit.shape[1]), jnp.bfloat16).at[slot_index].set(unit)]
    unnamed x0 -> x5, local copies, waits for them, and re-layouts: none -> 2.24 us
  transfers between devices with their start and end apart: 3 -> 0, of which waited for: 3 -> 0; matrix products, arithmetic and copies ran while one was open for 5% -> 0% of each run, Pallas kernels for 0% -> 0%
where the time goes in v1:
time: 56.1 us; the launch traced here: 55.8 us
  Pallas kernels  53.6 us (96%)
  local copies, waits for them, and re-layouts  2.24 us (4%)
    pallas_call x1, Pallas kernels, shards(): pl.pallas_call(kernel, out_shape=jax.ShapeDtypeStruct((1, ROWS), F32), in...  53.6 us
    unnamed x5, local copies, waits for them, and re-layouts  2.24 us

profile of v1, /device:TPU:1, one launch (start us, length us, event | category | flops | bytes accessed | tf_op | source)
XLA Modules:
  0.0 55.8 jit_solution(4156788662936967176)
XLA Ops:
  0.0 0.0 copy-start.1
  0.0 0.7 %copy-done.1 = s32[192]{0:T(256)S(1)} copy-done((s32[192]{0:T(256)S(1)}, s32[192]{0:T(256)}, u32[]{:S(2)}) %copy-start.1) | copy-done | bytes 792
  0.7 0.0 copy-start
  0.7 1.0 %copy-done = bf16[192,1024]{1,0:T(8,128)(2,1)S(1)} copy-done((bf16[192,1024]{1,0:T(8,128)(2,1)S(1)}, bf16[192,1024]{1,0:T(8,128)(2,1)}, u32[]{:S(2)}) %copy-start) | copy-done | bytes 393240
  1.7 53.6 %shard_map.28 = f32[1,192]{1,0:T(1,128)S(1)} custom-call(bf16[192,1024]{1,0:T(8,128)(2,1)S(1)} %copy-done, s32[1,192]{1,0:T(1,128)S(1)} %bitcast.3), custom_call_target="tpu_custom_call" | custom-call | tf_op jit(solution)/shard_map/pallas_call | solution.py:246
  55.2 0.6 %copy.4 = f32[192]{0:T(256)} copy(f32[192]{0:T(256)S(1)} %bitcast.2) | data formatting | bytes 1536
Async XLA Ops:
  0.0 0.7 %copy-start.1 = (s32[192]{0:T(256)S(1)}, s32[192]{0:T(256)}, u32[]{:S(2)}) copy-start(s32[192]{0:T(256)} %param.3) | copy-start | bytes 2308
  0.7 1.0 %copy-start = (bf16[192,1024]{1,0:T(8,128)(2,1)S(1)}, bf16[192,1024]{1,0:T(8,128)(2,1)}, u32[]{:S(2)}) copy-start(bf16[192,1024]{1,0:T(8,128)(2,1)} %emb_ref.1) | copy-start | bytes 1179652

commit v2 on v1

v2 whole, which is shorter than its diff:
```python
import functools
import math

import jax
import jax.numpy as jnp
from jax import lax
from jax.experimental import pallas as pl
from jax.experimental.pallas import tpu as pltpu
from jax.sharding import PartitionSpec as P

MESH = pl.DeviceIdType.MESH
F32, BF16, I32 = jnp.float32, jnp.bfloat16, jnp.int32

D = 1024
ROWS = 192
CAP = 12
OWNERS = 32
SLOTS = 64
CL_OWN = 32
QUARTERS = 4
QW = D // QUARTERS
BLK = QUARTERS * CAP
GRP = 16
NGRP = SLOTS // GRP
GROWS = GRP * CAP
HROWS = SLOTS * CAP
NT = 256
RETW = 256


def home_of(owner):
    y, z = owner // 8, lax.rem(owner // 2, 4)
    return lax.rem(y + z + 2 * lax.rem(owner, 2), 4), owner // 2


def shard_at(src, line):
    turn = lax.rem(src - line // 4 - lax.rem(line, 4) + 8, 4)
    return lax.rem(turn, 2) == 0, line * 2 + turn // 2


def div12(v):
    return (v * 5462) >> 16


def dot_nn(a, b):
    return lax.dot_general(a, b, (((1,), (0,)), ((), ())), preferred_element_type=F32)


def dot_nt(a, b):
    return lax.dot_general(a, b, (((1,), (1,)), ((), ())), preferred_element_type=F32)


def dot_tn(a, b):
    return lax.dot_general(a, b, (((0,), (0,)), ((), ())), preferred_element_type=F32)


def iota(shape, dim):
    return lax.broadcasted_iota(I32, shape, dim)


def swap_matrix():
    i, j = iota((GROWS, GROWS), 0), iota((GROWS, GROWS), 1)
    ab = div12(i)
    a, b = ab >> 2, ab & 3
    return (j == b * BLK + a * CAP + (i - ab * CAP)).astype(BF16)


def kernel(
    emb_hbm, ids_ref, out_ref,
    emb_ref, send, meta_send, recv, meta_recv, rows, theirs, meta_theirs, id_col, best, back,
    emb_sem, send_sem, meta_send_sem, recv_sem, meta_recv_sem, pass_sem, theirs_sem,
    meta_pass_sem, meta_theirs_sem, back_send_sem, back_sem,
):
    src, own = lax.axis_index("src"), lax.axis_index("own")
    line, core = own // 2, lax.rem(own, 2)
    is_home, shard = shard_at(src, line)
    slot = line * 4 + src
    partner = (src, own + 1 - 2 * core)

    barrier = pltpu.get_barrier_semaphore()
    fetch = pltpu.make_async_copy(emb_hbm, emb_ref, emb_sem)
    fetch.start()

    @pl.when(is_home)
    def _():
        pl.semaphore_signal(barrier, inc=1, device_id=partner, device_id_type=MESH)

        def greet(i, carry):
            to = lax.rem(slot + i, SLOTS)
            device = (lax.rem(to, 4), (to // 4) * 2 + core)
            pl.semaphore_signal(barrier, inc=1, device_id=device, device_id_type=MESH)
            return carry

        lax.fori_loop(1, SLOTS, greet, 0)

    ids = ids_ref[...]
    owner = ids >> 5
    onehot = iota((OWNERS, ROWS), 0) == owner
    onehot_b = onehot.astype(BF16)
    upto = (iota((ROWS, ROWS), 0) <= iota((ROWS, ROWS), 1)).astype(BF16)
    counts = dot_nn(onehot_b, upto)
    rank = jnp.sum(jnp.where(onehot, counts, 0.0), axis=0, keepdims=True).astype(I32) - 1
    place = owner * CAP + rank
    pick = (iota((OWNERS * CAP, ROWS), 0) == place).astype(BF16)

    local = (ids - owner * CL_OWN + 1).astype(F32)
    by_rank = jnp.where(iota((128, ROWS), 0) == rank, local, 0.0).astype(BF16)
    meta_send[...] = (dot_nt(onehot_b, by_rank) - 1.0).reshape(OWNERS, 1, 128)

    fetch.wait()
    values = emb_ref[...].astype(F32)
    mean = jnp.sum(values * values, axis=1, keepdims=True) * (1.0 / D)
    scale = lax.rsqrt(mean + 1e-06) * (1.0 / math.sqrt(D))
    unit = (values * scale).astype(BF16)
    packed = dot_nn(pick, unit).astype(BF16)
    swap = swap_matrix()
    for k in range(OWNERS // 4):
        part = packed[k * BLK : (k + 1) * BLK]
        stacked = jnp.concatenate([part[:, q * QW : (q + 1) * QW] for q in range(QUARTERS)], axis=0)
        send[pl.ds(4 * k, 4)] = dot_nn(swap, stacked).astype(BF16).reshape(4, BLK, QW)

    pl.semaphore_wait(barrier, OWNERS)

    def give_meta(i, carry):
        to = lax.rem(own + i, OWNERS)
        s, at = home_of(to)
        here = (s == src) & (at == line)

        @pl.when(jnp.logical_not(here))
        def _():
            pltpu.make_async_remote_copy(
                meta_send.at[to], meta_recv.at[slot], meta_send_sem, meta_recv_sem,
                device_id=(s, at * 2 + core), device_id_type=MESH,
            ).start()

        @pl.when(here)
        def _():
            pltpu.make_async_copy(meta_send.at[to], meta_recv.at[slot], meta_recv_sem).start()

        return carry

    lax.fori_loop(0, OWNERS, give_meta, 0)
    group = slot // GRP

    def give(i, carry):
        to = lax.rem(own + i, OWNERS)
        s, at = home_of(to)
        here = (s == src) & (at == line)

        @pl.when(jnp.logical_not(here))
        def _():
            pltpu.make_async_remote_copy(
                send.at[to], recv.at[slot], send_sem, recv_sem.at[group],
                device_id=(s, at * 2 + core), device_id_type=MESH,
            ).start()

        @pl.when(here)
        def _():
            pltpu.make_async_copy(send.at[to], recv.at[slot], recv_sem.at[group]).start()

        return carry

    lax.fori_loop(0, OWNERS, give, 0)

    @pl.when(is_home)
    def _():
        lane_of = iota((GRP, GROWS), 1)
        spread = (div12(lane_of) == iota((GRP, GROWS), 0)).astype(BF16)
        nth_row = iota((GRP, GROWS), 0) == lane_of - div12(lane_of) * CAP
        sub = iota((GROWS, 128), 0)
        nth_col = iota((GROWS, 128), 1) == sub - div12(sub) * CAP

        pltpu.make_async_copy(meta_recv, meta_recv, meta_recv_sem).wait()
        meta_pass = pltpu.make_async_remote_copy(
            meta_recv, meta_theirs, meta_pass_sem, meta_theirs_sem,
            device_id=partner, device_id_type=MESH,
        )
        meta_pass.start()

        def down(ref, g):
            ids_g = ref[pl.ds(g * GRP, GRP)].reshape(GRP, 128).astype(BF16)
            wide = dot_tn(spread, ids_g)
            return ids_g, jnp.sum(jnp.where(nth_col, wide, 0.0), axis=1, keepdims=True)

        along = []
        for g in range(NGRP):
            ids_g, col_g = down(meta_recv, g)
            id_col[0, g * GROWS : (g + 1) * GROWS] = col_g
            wide = dot_tn(ids_g, spread)[:GRP]
            along.append(jnp.sum(jnp.where(nth_row, wide, 0.0), axis=0, keepdims=True))
        along = jnp.concatenate(along, axis=1)
        meta_pass.wait_recv()
        for g in range(NGRP):
            id_col[1, g * GROWS : (g + 1) * GROWS] = down(meta_theirs, g)[1]

        def passing(g):
            part = pl.ds(g * GROWS, GROWS)
            return pltpu.make_async_remote_copy(
                rows.at[part], theirs.at[part], pass_sem, theirs_sem,
                device_id=partner, device_id_type=MESH,
            )

        for g in range(NGRP):
            block = recv.at[pl.ds(g * GRP, GRP)]
            pltpu.make_async_copy(block, block, recv_sem.at[g]).wait()
            for k in range(GRP // 4):
                four = recv[pl.ds(g * GRP + 4 * k, 4)].reshape(GROWS, QW)
                turned = dot_nn(swap, four).astype(BF16)
                at = g * GROWS + k * BLK
                for q in range(QUARTERS):
                    rows[at : at + BLK, q * QW : (q + 1) * QW] = turned[q * BLK : (q + 1) * BLK]
            passing(g).start()

        found = []
        for n in range(HROWS // NT):
            mine = rows[n * NT : (n + 1) * NT, :]
            scores = dot_nt(rows[...], mine)
            keep = (id_col[0] == along[:, n * NT : (n + 1) * NT]) & (
                iota((HROWS, NT), 0) != iota((HROWS, NT), 1) + n * NT
            )
            found.append(jnp.max(jnp.where(keep, scores, -1.0), axis=0, keepdims=True))
        pltpu.make_async_copy(theirs, theirs, theirs_sem).wait()
        for n in range(HROWS // NT):
            mine = rows[n * NT : (n + 1) * NT, :]
            scores = dot_nt(theirs[...], mine)
            keep = id_col[1] == along[:, n * NT : (n + 1) * NT]
            top = jnp.max(jnp.where(keep, scores, -1.0), axis=0, keepdims=True)
            found[n] = jnp.maximum(jnp.maximum(found[n], top), -1.0)
        found = jnp.concatenate(found, axis=1)
        for g in range(NGRP):
            best[g, :, :GROWS] = found[:, g * GROWS : (g + 1) * GROWS]

        def give_back(to, carry):
            @pl.when(to != slot)
            def _():
                pltpu.make_async_remote_copy(
                    best.at[to // GRP], back.at[shard], back_send_sem, back_sem,
                    device_id=(lax.rem(to, 4), (to // 4) * 2 + core), device_id_type=MESH,
                ).start()

            @pl.when(to == slot)
            def _():
                pltpu.make_async_copy(best.at[group], back.at[shard], back_sem).start()

            return carry

        lax.fori_loop(0, SLOTS, give_back, 0)

    pltpu.make_async_copy(back, back, back_sem).wait()
    got = back[...].reshape(OWNERS, RETW)
    high = got.astype(BF16)
    rest = got - high.astype(F32)
    mid = rest.astype(BF16)
    low = (rest - mid.astype(F32)).astype(BF16)
    wide = dot_tn(high, onehot_b) + dot_tn(mid, onehot_b) + dot_tn(low, onehot_b)
    lane = lax.rem(slot, GRP) * CAP + rank
    out_ref[...] = jnp.sum(jnp.where(iota((RETW, ROWS), 0) == lane, wide, 0.0), axis=0, keepdims=True)

    @pl.when(is_home)
    def _():
        part = send.at[pl.ds(0, OWNERS - 1)]
        pltpu.make_async_copy(part, part, send_sem).wait()
        part = meta_send.at[pl.ds(0, OWNERS - 1)]
        pltpu.make_async_copy(part, part, meta_send_sem).wait()
        pltpu.make_async_copy(meta_recv, meta_recv, meta_pass_sem).wait()
        pltpu.make_async_copy(rows, rows, pass_sem).wait()
        pltpu.make_async_copy(back, back, back_send_sem).wait()
        part = back.at[pl.ds(0, OWNERS - 1)]
        pltpu.make_async_copy(part, part, back_send_sem).wait()

    @pl.when(jnp.logical_not(is_home))
    def _():
        pltpu.make_async_copy(send, send, send_sem).wait()
        pltpu.make_async_copy(meta_send, meta_send, meta_send_sem).wait()


def shards(embeddings, cluster_ids):
    dma = pltpu.SemaphoreType.DMA
    out = pl.pallas_call(
        kernel,
        out_shape=jax.ShapeDtypeStruct((1, ROWS), F32),
        in_specs=[pl.BlockSpec(memory_space=pl.ANY), pl.BlockSpec(memory_space=pltpu.VMEM)],
        out_specs=pl.BlockSpec(memory_space=pltpu.VMEM),
        scratch_shapes=[
            pltpu.VMEM((ROWS, D), BF16),
            pltpu.VMEM((OWNERS, BLK, QW), BF16),
            pltpu.VMEM((OWNERS, 1, 128), F32),
            pltpu.VMEM((SLOTS, BLK, QW), BF16),
            pltpu.VMEM((SLOTS, 1, 128), F32),
            pltpu.VMEM((HROWS, D), BF16),
            pltpu.VMEM((HROWS, D), BF16),
            pltpu.VMEM((SLOTS, 1, 128), F32),
            pltpu.VMEM((2, HROWS, 1), F32),
            pltpu.VMEM((NGRP, 1, RETW), F32),
            pltpu.VMEM((OWNERS, 1, RETW), F32),
            dma, dma, dma, dma((NGRP,)), dma, dma, dma, dma, dma, dma, dma,
        ],
        compiler_params=pltpu.CompilerParams(
            collective_id=0, has_side_effects=True, vmem_limit_bytes=40 << 20
        ),
    )(embeddings, cluster_ids.reshape(1, ROWS))
    return out.reshape(ROWS)


def solution(mesh):
    in_specs = (P(("src", "own"), None), P(("src", "own")))
    out_specs = P(("src", "own"))
    return jax.shard_map(shards, mesh=mesh, in_specs=in_specs, out_specs=out_specs, check_vma=False)
```

time: 56.1 us -> 42.8 us (0.76)
  Pallas kernels: 53.6 us -> 40.4 us
    pallas_call x1, Pallas kernels: 53.6 us -> 40.4 us  [shards(): pl.pallas_call(kernel, out_shape=jax.ShapeDtypeStruct((1, ROWS), F32), in...]
where the time goes in v2:
time: 42.8 us; the launch traced here: 42.6 us
  Pallas kernels  40.4 us (94%)
  local copies, waits for them, and re-layouts  2.24 us (5%)
    pallas_call x1, Pallas kernels, shards(): pl.pallas_call(kernel, out_shape=jax.ShapeDtypeStruct((1, ROWS), F32), in...  40.4 us
    unnamed x5, local copies, waits for them, and re-layouts  2.24 us

profile of v2, /device:TPU:1, one launch (start us, length us, event | category | flops | bytes accessed | tf_op | source)
XLA Modules:
  0.0 42.6 jit_solution(9367858509799431764)
XLA Ops:
  0.0 0.0 copy-start.1
  0.0 0.7 %copy-done.1 = s32[192]{0:T(256)S(1)} copy-done((s32[192]{0:T(256)S(1)}, s32[192]{0:T(256)}, u32[]{:S(2)}) %copy-start.1) | copy-done | bytes 792
  0.7 0.0 copy-start
  0.7 1.0 %copy-done = bf16[192,1024]{1,0:T(8,128)(2,1)S(1)} copy-done((bf16[192,1024]{1,0:T(8,128)(2,1)S(1)}, bf16[192,1024]{1,0:T(8,128)(2,1)}, u32[]{:S(2)}) %copy-start) | copy-done | bytes 393240
  1.7 40.4 %shard_map.28 = f32[1,192]{1,0:T(1,128)S(1)} custom-call(bf16[192,1024]{1,0:T(8,128)(2,1)S(1)} %copy-done, s32[1,192]{1,0:T(1,128)S(1)} %bitcast.3), custom_call_target="tpu_custom_call" | custom-call | tf_op jit(solution)/shard_map/pallas_call | solution.py:279
  42.1 0.6 %copy.4 = f32[192]{0:T(256)} copy(f32[192]{0:T(256)S(1)} %bitcast.2) | data formatting | bytes 1536
Async XLA Ops:
  0.0 0.7 %copy-start.1 = (s32[192]{0:T(256)S(1)}, s32[192]{0:T(256)}, u32[]{:S(2)}) copy-start(s32[192]{0:T(256)} %param.3) | copy-start | bytes 2308
  0.7 1.0 %copy-start = (bf16[192,1024]{1,0:T(8,128)(2,1)S(1)}, bf16[192,1024]{1,0:T(8,128)(2,1)}, u32[]{:S(2)}) copy-start(bf16[192,1024]{1,0:T(8,128)(2,1)} %emb_hbm.1) | copy-start | bytes 1179652

commit v3 on v2

--- a/solution.py
+++ b/solution.py
@@ -29,13 +29,15 @@
 
 
 def home_of(owner):
-    y, z = owner // 8, lax.rem(owner // 2, 4)
-    return lax.rem(y + z + 2 * lax.rem(owner, 2), 4), owner // 2
-
-
-def shard_at(src, line):
-    turn = lax.rem(src - line // 4 - lax.rem(line, 4) + 8, 4)
-    return lax.rem(turn, 2) == 0, line * 2 + turn // 2
+    return lax.rem(owner, 4), lax.rem(owner // 4, 4), (owner // 16) * 2
+
+
+def gray(v):
+    return v + v // 2 - 2 * (v // 3)
+
+
+def at(x, y, z, core):
+    return x, y * 8 + z * 2 + core
 
 
 def div12(v):
@@ -72,9 +74,10 @@
     meta_pass_sem, meta_theirs_sem, back_send_sem, back_sem,
 ):
     src, own = lax.axis_index("src"), lax.axis_index("own")
-    line, core = own // 2, lax.rem(own, 2)
-    is_home, shard = shard_at(src, line)
-    slot = line * 4 + src
+    y, z, core = own // 8, lax.rem(own // 2, 4), lax.rem(own, 2)
+    is_home, shard = lax.rem(z, 2) == 0, (z // 2) * 16 + y * 4 + src
+    is_relay = (lax.rem(z, 2) == 1) & (core == 1)
+    seat = y * 4 + src
     partner = (src, own + 1 - 2 * core)
 
     barrier = pltpu.get_barrier_semaphore()
@@ -86,12 +89,21 @@
         pl.semaphore_signal(barrier, inc=1, device_id=partner, device_id_type=MESH)
 
         def greet(i, carry):
-            to = lax.rem(slot + i, SLOTS)
-            device = (lax.rem(to, 4), (to // 4) * 2 + core)
+            to = lax.rem(z * 16 + seat + i, SLOTS)
+            device = at(lax.rem(to, 4), lax.rem(to // 4, 4), to // 16, core)
             pl.semaphore_signal(barrier, inc=1, device_id=device, device_id_type=MESH)
             return carry
 
         lax.fori_loop(1, SLOTS, greet, 0)
+
+    @pl.when(is_relay)
+    def _():
+        def greet(i, carry):
+            device = at(lax.rem(i, 4), i // 4, lax.rem(z + 1, 4), core)
+            pl.semaphore_signal(barrier, inc=1, device_id=device, device_id_type=MESH)
+            return carry
+
+        lax.fori_loop(0, GRP, greet, 0)
 
     ids = ids_ref[...]
     owner = ids >> 5
@@ -119,18 +131,32 @@
         stacked = jnp.concatenate([part[:, q * QW : (q + 1) * QW] for q in range(QUARTERS)], axis=0)
         send[pl.ds(4 * k, 4)] = dot_nn(swap, stacked).astype(BF16).reshape(4, BLK, QW)
 
-    pl.semaphore_wait(barrier, OWNERS)
+    @pl.when(is_home & (core == 1))
+    def _():
+        pl.semaphore_wait(barrier, OWNERS + GRP)
+
+    @pl.when(jnp.logical_not(is_home & (core == 1)))
+    def _():
+        pl.semaphore_wait(barrier, OWNERS)
+
+    plane = lax.rem(z // 2 + core, 2)
+
+    def target(i):
+        to = lax.rem(plane + i // 16, 2) * 16 + lax.rem(seat + i, 16)
+        hx, hy, hz = home_of(to)
+        away = lax.rem(z - hz + 4, 4)
+        here = (hx == src) & (hy == y) & (away == 0)
+        return to, hx, hy, hz, away, here, gray(away)
 
     def give_meta(i, carry):
-        to = lax.rem(own + i, OWNERS)
-        s, at = home_of(to)
-        here = (s == src) & (at == line)
+        to, hx, hy, hz, away, here, group = target(i)
+        slot = group * GRP + seat
 
         @pl.when(jnp.logical_not(here))
         def _():
             pltpu.make_async_remote_copy(
                 meta_send.at[to], meta_recv.at[slot], meta_send_sem, meta_recv_sem,
-                device_id=(s, at * 2 + core), device_id_type=MESH,
+                device_id=at(hx, hy, hz, core), device_id_type=MESH,
             ).start()
 
         @pl.when(here)
@@ -140,18 +166,24 @@
         return carry
 
     lax.fori_loop(0, OWNERS, give_meta, 0)
-    group = slot // GRP
 
     def give(i, carry):
-        to = lax.rem(own + i, OWNERS)
-        s, at = home_of(to)
-        here = (s == src) & (at == line)
-
-        @pl.when(jnp.logical_not(here))
+        to, hx, hy, hz, away, here, group = target(i)
+        slot = group * GRP + seat
+        via = (away == 2) & (core == 1)
+
+        @pl.when(via)
+        def _():
+            pltpu.make_async_remote_copy(
+                send.at[to], recv.at[seat], send_sem, recv_sem.at[y],
+                device_id=at(hx, hy, hz + 1, core), device_id_type=MESH,
+            ).start()
+
+        @pl.when(jnp.logical_not(here | via))
         def _():
             pltpu.make_async_remote_copy(
                 send.at[to], recv.at[slot], send_sem, recv_sem.at[group],
-                device_id=(s, at * 2 + core), device_id_type=MESH,
+                device_id=at(hx, hy, hz, core), device_id_type=MESH,
             ).start()
 
         @pl.when(here)
@@ -161,6 +193,19 @@
         return carry
 
     lax.fori_loop(0, OWNERS, give, 0)
+
+    def onward(k):
+        return pltpu.make_async_remote_copy(
+            recv.at[pl.ds(4 * k, 4)], recv.at[pl.ds(3 * GRP + 4 * k, 4)], pass_sem, recv_sem.at[3],
+            device_id=at(src, y, z - 1, core), device_id_type=MESH,
+        )
+
+    @pl.when(is_relay)
+    def _():
+        for k in range(4):
+            block = recv.at[pl.ds(4 * k, 4)]
+            pltpu.make_async_copy(block, block, recv_sem.at[k]).wait()
+            onward(k).start()
 
     @pl.when(is_home)
     def _():
@@ -206,9 +251,9 @@
             for k in range(GRP // 4):
                 four = recv[pl.ds(g * GRP + 4 * k, 4)].reshape(GROWS, QW)
                 turned = dot_nn(swap, four).astype(BF16)
-                at = g * GROWS + k * BLK
+                first = g * GROWS + k * BLK
                 for q in range(QUARTERS):
-                    rows[at : at + BLK, q * QW : (q + 1) * QW] = turned[q * BLK : (q + 1) * BLK]
+                    rows[first : first + BLK, q * QW : (q + 1) * QW] = turned[q * BLK : (q + 1) * BLK]
             passing(g).start()
 
         found = []
@@ -231,16 +276,17 @@
             best[g, :, :GROWS] = found[:, g * GROWS : (g + 1) * GROWS]
 
         def give_back(to, carry):
-            @pl.when(to != slot)
+            @pl.when(to != seat)
             def _():
+                device = at(lax.rem(to, 4), lax.rem(to // 4, 4), lax.rem(z + gray(to // GRP), 4), core)
                 pltpu.make_async_remote_copy(
                     best.at[to // GRP], back.at[shard], back_send_sem, back_sem,
-                    device_id=(lax.rem(to, 4), (to // 4) * 2 + core), device_id_type=MESH,
+                    device_id=device, device_id_type=MESH,
                 ).start()
 
-            @pl.when(to == slot)
+            @pl.when(to == seat)
             def _():
-                pltpu.make_async_copy(best.at[group], back.at[shard], back_sem).start()
+                pltpu.make_async_copy(best.at[0], back.at[shard], back_sem).start()
 
             return carry
 
@@ -253,7 +299,7 @@
     mid = rest.astype(BF16)
     low = (rest - mid.astype(F32)).astype(BF16)
     wide = dot_tn(high, onehot_b) + dot_tn(mid, onehot_b) + dot_tn(low, onehot_b)
-    lane = lax.rem(slot, GRP) * CAP + rank
+    lane = seat * CAP + rank
     out_ref[...] = jnp.sum(jnp.where(iota((RETW, ROWS), 0) == lane, wide, 0.0), axis=0, keepdims=True)
 
     @pl.when(is_home)
@@ -272,6 +318,11 @@
     def _():
         pltpu.make_async_copy(send, send, send_sem).wait()
         pltpu.make_async_copy(meta_send, meta_send, meta_send_sem).wait()
+
+    @pl.when(is_relay)
+    def _():
+        part = recv.at[pl.ds(0, GRP)]
+        pltpu.make_async_copy(part, part, pass_sem).wait()
 
 
 def shards(embeddings, cluster_ids):

time: 42.8 us -> 39.7 us (0.928)
  Pallas kernels: 40.4 us -> 37.2 us
    pallas_call x1, Pallas kernels: 40.4 us -> 37.2 us  [shards(): pl.pallas_call(kernel, out_shape=jax.ShapeDtypeStruct((1, ROWS), F32), in...]
where the time goes in v3:
time: 39.7 us; the launch traced here: 39.5 us
  Pallas kernels  37.2 us (94%)
  local copies, waits for them, and re-layouts  2.24 us (6%)
    pallas_call x1, Pallas kernels, shards(): pl.pallas_call(kernel, out_shape=jax.ShapeDtypeStruct((1, ROWS), F32), in...  37.2 us
    unnamed x5, local copies, waits for them, and re-layouts  2.24 us

profile of v3, /device:TPU:1, one launch (start us, length us, event | category | flops | bytes accessed | tf_op | source)
XLA Modules:
  0.0 39.5 jit_solution(804138332358939319)
XLA Ops:
  0.0 0.0 copy-start.1
  0.0 0.7 %copy-done.1 = s32[192]{0:T(256)S(1)} copy-done((s32[192]{0:T(256)S(1)}, s32[192]{0:T(256)}, u32[]{:S(2)}) %copy-start.1) | copy-done | bytes 792
  0.7 0.0 copy-start
  0.7 1.0 %copy-done = bf16[192,1024]{1,0:T(8,128)(2,1)S(1)} copy-done((bf16[192,1024]{1,0:T(8,128)(2,1)S(1)}, bf16[192,1024]{1,0:T(8,128)(2,1)}, u32[]{:S(2)}) %copy-start) | copy-done | bytes 393240
  1.7 37.2 %shard_map.28 = f32[1,192]{1,0:T(1,128)S(1)} custom-call(bf16[192,1024]{1,0:T(8,128)(2,1)S(1)} %copy-done, s32[1,192]{1,0:T(1,128)S(1)} %bitcast.3), custom_call_target="tpu_custom_call" | custom-call | tf_op jit(solution)/shard_map/pallas_call | solution.py:330
  38.9 0.6 %copy.4 = f32[192]{0:T(256)} copy(f32[192]{0:T(256)S(1)} %bitcast.2) | data formatting | bytes 1536
Async XLA Ops:
  0.0 0.7 %copy-start.1 = (s32[192]{0:T(256)S(1)}, s32[192]{0:T(256)}, u32[]{:S(2)}) copy-start(s32[192]{0:T(256)} %param.3) | copy-start | bytes 2308
  0.7 1.0 %copy-start = (bf16[192,1024]{1,0:T(8,128)(2,1)S(1)}, bf16[192,1024]{1,0:T(8,128)(2,1)}, u32[]{:S(2)}) copy-start(bf16[192,1024]{1,0:T(8,128)(2,1)} %emb_hbm.1) | copy-start | bytes 1179652

commit v4 on v3

--- a/solution.py
+++ b/solution.py
@@ -24,7 +24,7 @@
 NGRP = SLOTS // GRP
 GROWS = GRP * CAP
 HROWS = SLOTS * CAP
-NT = 256
+HALF = HROWS // 2
 RETW = 256
 
 
@@ -68,9 +68,9 @@
 
 
 def kernel(
-    emb_hbm, ids_ref, out_ref,
-    emb_ref, send, meta_send, recv, meta_recv, rows, theirs, meta_theirs, id_col, best, back,
-    emb_sem, send_sem, meta_send_sem, recv_sem, meta_recv_sem, pass_sem, theirs_sem,
+    emb_hbm, ids_hbm, out_ref,
+    emb_ref, ids_ref, send, meta_send, recv, meta_recv, rows, theirs, meta_theirs, id_col, best, back,
+    emb_sem, ids_sem, send_sem, meta_send_sem, recv_sem, meta_recv_sem, pass_sem, theirs_sem,
     meta_pass_sem, meta_theirs_sem, back_send_sem, back_sem,
 ):
     src, own = lax.axis_index("src"), lax.axis_index("own")
@@ -82,6 +82,8 @@
 
     barrier = pltpu.get_barrier_semaphore()
     fetch = pltpu.make_async_copy(emb_hbm, emb_ref, emb_sem)
+    fetch_ids = pltpu.make_async_copy(ids_hbm, ids_ref, ids_sem)
+    fetch_ids.start()
     fetch.start()
 
     @pl.when(is_home)
@@ -105,6 +107,7 @@
 
         lax.fori_loop(0, GRP, greet, 0)
 
+    fetch_ids.wait()
     ids = ids_ref[...]
     owner = ids >> 5
     onehot = iota((OWNERS, ROWS), 0) == owner
@@ -165,7 +168,6 @@
 
         return carry
 
-    lax.fori_loop(0, OWNERS, give_meta, 0)
 
     def give(i, carry):
         to, hx, hy, hz, away, here, group = target(i)
@@ -192,7 +194,9 @@
 
         return carry
 
-    lax.fori_loop(0, OWNERS, give, 0)
+    lax.fori_loop(0, 8, give, 0)
+    lax.fori_loop(0, OWNERS, give_meta, 0)
+    lax.fori_loop(8, OWNERS, give, 0)
 
     def onward(k):
         return pltpu.make_async_remote_copy(
@@ -241,11 +245,11 @@
         def passing(g):
             part = pl.ds(g * GROWS, GROWS)
             return pltpu.make_async_remote_copy(
-                rows.at[part], theirs.at[part], pass_sem, theirs_sem,
+                rows.at[part], theirs.at[part], pass_sem, theirs_sem.at[g // 2],
                 device_id=partner, device_id_type=MESH,
             )
 
-        for g in range(NGRP):
+        def turn(g):
             block = recv.at[pl.ds(g * GRP, GRP)]
             pltpu.make_async_copy(block, block, recv_sem.at[g]).wait()
             for k in range(GRP // 4):
@@ -256,41 +260,53 @@
                     rows[first : first + BLK, q * QW : (q + 1) * QW] = turned[q * BLK : (q + 1) * BLK]
             passing(g).start()
 
-        found = []
-        for n in range(HROWS // NT):
-            mine = rows[n * NT : (n + 1) * NT, :]
-            scores = dot_nt(rows[...], mine)
-            keep = (id_col[0] == along[:, n * NT : (n + 1) * NT]) & (
-                iota((HROWS, NT), 0) != iota((HROWS, NT), 1) + n * NT
-            )
-            found.append(jnp.max(jnp.where(keep, scores, -1.0), axis=0, keepdims=True))
-        pltpu.make_async_copy(theirs, theirs, theirs_sem).wait()
-        for n in range(HROWS // NT):
-            mine = rows[n * NT : (n + 1) * NT, :]
-            scores = dot_nt(theirs[...], mine)
-            keep = id_col[1] == along[:, n * NT : (n + 1) * NT]
-            top = jnp.max(jnp.where(keep, scores, -1.0), axis=0, keepdims=True)
-            found[n] = jnp.maximum(jnp.maximum(found[n], top), -1.0)
-        found = jnp.concatenate(found, axis=1)
-        for g in range(NGRP):
-            best[g, :, :GROWS] = found[:, g * GROWS : (g + 1) * GROWS]
-
-        def give_back(to, carry):
-            @pl.when(to != seat)
-            def _():
-                device = at(lax.rem(to, 4), lax.rem(to // 4, 4), lax.rem(z + gray(to // GRP), 4), core)
-                pltpu.make_async_remote_copy(
-                    best.at[to // GRP], back.at[shard], back_send_sem, back_sem,
-                    device_id=device, device_id_type=MESH,
-                ).start()
-
-            @pl.when(to == seat)
-            def _():
+        def top(ref, side, down_at, along_at):
+            mine = rows[along_at : along_at + HALF, :]
+            scores = dot_nt(ref[down_at : down_at + HALF, :], mine)
+            keep = id_col[side, down_at : down_at + HALF] == along[:, along_at : along_at + HALF]
+            if side == 0 and down_at == along_at:
+                keep &= iota((HALF, HALF), 0) != iota((HALF, HALF), 1)
+            return jnp.max(jnp.where(keep, scores, -1.0), axis=0, keepdims=True)
+
+        def arrived(half):
+            part = theirs.at[pl.ds(half * HALF, HALF)]
+            pltpu.make_async_copy(part, part, theirs_sem.at[half]).wait()
+
+        def give_back(g, found):
+            best[g, :, :GROWS] = found
+            for to in range(GRP):
+                device = at(to % 4, to // 4, lax.rem(z + gray(g), 4), core)
+
+                def one(device=device):
+                    pltpu.make_async_remote_copy(
+                        best.at[g], back.at[shard], back_send_sem, back_sem,
+                        device_id=device, device_id_type=MESH,
+                    ).start()
+
+                if g:
+                    one()
+                else:
+                    pl.when(to != seat)(one)
+            if g == 0:
                 pltpu.make_async_copy(best.at[0], back.at[shard], back_sem).start()
 
-            return carry
-
-        lax.fori_loop(0, SLOTS, give_back, 0)
+        turn(0)
+        turn(1)
+        first = top(rows, 0, 0, 0)
+        arrived(0)
+        first = jnp.maximum(first, top(theirs, 1, 0, 0))
+        turn(2)
+        turn(3)
+        second = jnp.maximum(top(rows, 0, 0, HALF), top(rows, 0, HALF, HALF))
+        second = jnp.maximum(second, top(theirs, 1, 0, HALF))
+        first = jnp.maximum(first, top(rows, 0, HALF, 0))
+        arrived(1)
+        first = jnp.maximum(jnp.maximum(first, top(theirs, 1, HALF, 0)), -1.0)
+        give_back(0, first[:, :GROWS])
+        give_back(1, first[:, GROWS:])
+        second = jnp.maximum(jnp.maximum(second, top(theirs, 1, HALF, HALF)), -1.0)
+        give_back(2, second[:, :GROWS])
+        give_back(3, second[:, GROWS:])
 
     pltpu.make_async_copy(back, back, back_sem).wait()
     got = back[...].reshape(OWNERS, RETW)
@@ -330,10 +346,11 @@
     out = pl.pallas_call(
         kernel,
         out_shape=jax.ShapeDtypeStruct((1, ROWS), F32),
-        in_specs=[pl.BlockSpec(memory_space=pl.ANY), pl.BlockSpec(memory_space=pltpu.VMEM)],
+        in_specs=[pl.BlockSpec(memory_space=pltpu.HBM)] * 2,
         out_specs=pl.BlockSpec(memory_space=pltpu.VMEM),
         scratch_shapes=[
             pltpu.VMEM((ROWS, D), BF16),
+            pltpu.VMEM((1, ROWS), I32),
             pltpu.VMEM((OWNERS, BLK, QW), BF16),
             pltpu.VMEM((OWNERS, 1, 128), F32),
             pltpu.VMEM((SLOTS, BLK, QW), BF16),
@@ -344,10 +361,10 @@
             pltpu.VMEM((2, HROWS, 1), F32),
             pltpu.VMEM((NGRP, 1, RETW), F32),
             pltpu.VMEM((OWNERS, 1, RETW), F32),
-            dma, dma, dma, dma((NGRP,)), dma, dma, dma, dma, dma, dma, dma,
+            dma, dma, dma, dma, dma((NGRP,)), dma, dma, dma((2,)), dma, dma, dma, dma,
         ],
         compiler_params=pltpu.CompilerParams(
-            collective_id=0, has_side_effects=True, vmem_limit_bytes=40 << 20
+            collective_id=0, has_side_effects=True, vmem_limit_bytes=60 << 20
         ),
     )(embeddings, cluster_ids.reshape(1, ROWS))
     return out.reshape(ROWS)

time: 39.7 us -> 36.3 us (0.914)
  Pallas kernels: 37.2 us -> 35 us
  local copies, waits for them, and re-layouts: 2.24 us -> 1.22 us
    pallas_call x1, Pallas kernels: 37.2 us -> 35 us  [shards(): pl.pallas_call(kernel, out_shape=jax.ShapeDtypeStruct((1, ROWS), F32), in...]
    unnamed x5 -> x3, local copies, waits for them, and re-layouts: 2.24 us -> 1.22 us
where the time goes in v4:
time: 36.3 us; the launch traced here: 36.2 us
  Pallas kernels  35 us (96%)
  local copies, waits for them, and re-layouts  1.22 us (3%)
    pallas_call x1, Pallas kernels, shards(): pl.pallas_call(kernel, out_shape=jax.ShapeDtypeStruct((1, ROWS), F32), in...  35 us
    unnamed x3, local copies, waits for them, and re-layouts  1.22 us

profile of v4, /device:TPU:1, one launch (start us, length us, event | category | flops | bytes accessed | tf_op | source)
XLA Modules:
  0.0 36.2 jit_solution(11317859602092137972)
XLA Ops:
  0.0 35.0 %shard_map.28 = f32[1,192]{1,0:T(1,128)} custom-call(bf16[192,1024]{1,0:T(8,128)(2,1)} %emb_hbm.1, s32[1,192]{1,0:T(1,128)} %bitcast.3), custom_call_target="tpu_custom_call" | custom-call | tf_op jit(solution)/shard_map/pallas_call | solution.py:346
  35.0 0.0 copy-start
  35.0 0.7 %copy-done = f32[1,192]{1,0:T(1,128)S(1)} copy-done((f32[1,192]{1,0:T(1,128)S(1)}, f32[1,192]{1,0:T(1,128)}, u32[]{:S(2)}) %copy-start) | copy-done | bytes 792
  35.7 0.6 %copy.4 = f32[192]{0:T(256)} copy(f32[192]{0:T(256)S(1)} %bitcast.2) | data formatting | bytes 1536
Async XLA Ops:
  35.0 0.7 %copy-start = (f32[1,192]{1,0:T(1,128)S(1)}, f32[1,192]{1,0:T(1,128)}, u32[]{:S(2)}) copy-start(f32[1,192]{1,0:T(1,128)} %shard_map.28) | copy-start | bytes 2308

commit v5 on v4

--- a/solution.py
+++ b/solution.py
@@ -33,7 +33,7 @@
 
 
 def gray(v):
-    return v + v // 2 - 2 * (v // 3)
+    return v + (v // 2) * (1 - 2 * lax.rem(v, 2))
 
 
 def at(x, y, z, core):
@@ -144,59 +144,64 @@
 
     plane = lax.rem(z // 2 + core, 2)
 
-    def target(i):
-        to = lax.rem(plane + i // 16, 2) * 16 + lax.rem(seat + i, 16)
-        hx, hy, hz = home_of(to)
-        away = lax.rem(z - hz + 4, 4)
-        here = (hx == src) & (hy == y) & (away == 0)
-        return to, hx, hy, hz, away, here, gray(away)
-
-    def give_meta(i, carry):
-        to, hx, hy, hz, away, here, group = target(i)
-        slot = group * GRP + seat
-
-        @pl.when(jnp.logical_not(here))
-        def _():
+    def send_one(source, landed, device, sent, arrived, here):
+        def away():
             pltpu.make_async_remote_copy(
-                meta_send.at[to], meta_recv.at[slot], meta_send_sem, meta_recv_sem,
-                device_id=at(hx, hy, hz, core), device_id_type=MESH,
+                source, landed, sent, arrived, device_id=device, device_id_type=MESH
             ).start()
 
-        @pl.when(here)
-        def _():
-            pltpu.make_async_copy(meta_send.at[to], meta_recv.at[slot], meta_recv_sem).start()
-
-        return carry
-
-
-    def give(i, carry):
-        to, hx, hy, hz, away, here, group = target(i)
-        slot = group * GRP + seat
-        via = (away == 2) & (core == 1)
-
-        @pl.when(via)
-        def _():
-            pltpu.make_async_remote_copy(
-                send.at[to], recv.at[seat], send_sem, recv_sem.at[y],
-                device_id=at(hx, hy, hz + 1, core), device_id_type=MESH,
-            ).start()
-
-        @pl.when(jnp.logical_not(here | via))
-        def _():
-            pltpu.make_async_remote_copy(
-                send.at[to], recv.at[slot], send_sem, recv_sem.at[group],
-                device_id=at(hx, hy, hz, core), device_id_type=MESH,
-            ).start()
-
-        @pl.when(here)
-        def _():
-            pltpu.make_async_copy(send.at[to], recv.at[slot], recv_sem.at[group]).start()
-
-        return carry
-
-    lax.fori_loop(0, 8, give, 0)
-    lax.fori_loop(0, OWNERS, give_meta, 0)
-    lax.fori_loop(8, OWNERS, give, 0)
+        if here is None:
+            away()
+        else:
+            pl.when(jnp.logical_not(here))(away)
+            pl.when(here)(lambda: pltpu.make_async_copy(source, landed, arrived).start())
+
+    def half(p):
+        hz = 2 * lax.rem(plane + p, 2)
+        above = lax.rem(z - hz + 4, 4)
+        group = gray(above)
+        via = core * (above // 2) * (1 - lax.rem(above, 2))
+        landing = seat + GRP * group * (1 - via)
+        signal = group + via * (y - group)
+
+        def place(j):
+            if isinstance(j, int):
+                dx, dy = (0, 1, 3, 2)[j % 4], (0, 1, 3, 2)[j // 4]
+            else:
+                dx, dy = gray(lax.rem(j, 4)), gray(j // 4)
+            hx, hy = lax.rem(src + dx, 4), lax.rem(y + dy, 4)
+            here = (above == 0) if isinstance(j, int) and j == 0 else None
+            return hx, hy, 8 * hz + 4 * hy + hx, here
+
+        def give(j, carry):
+            hx, hy, to, here = place(j)
+            send_one(
+                send.at[to], recv.at[landing], at(hx, hy, hz + via, core), send_sem, recv_sem.at[signal], here
+            )
+            return carry
+
+        def give_meta(j, carry):
+            hx, hy, to, here = place(j)
+            send_one(
+                meta_send.at[to], meta_recv.at[GRP * group + seat], at(hx, hy, hz, core),
+                meta_send_sem, meta_recv_sem, here,
+            )
+            return carry
+
+        return give, give_meta
+
+    def run(f, first, last):
+        if first == 0:
+            f(0, 0)
+        lax.fori_loop(max(first, 1), last, f, 0, unroll=False)
+
+    rows_a, ids_a = half(0)
+    rows_b, ids_b = half(1)
+    run(rows_a, 0, 8)
+    run(ids_a, 0, GRP)
+    run(ids_b, 0, GRP)
+    run(rows_a, 8, GRP)
+    run(rows_b, 0, GRP)
 
     def onward(k):
         return pltpu.make_async_remote_copy(
@@ -275,7 +280,7 @@
         def give_back(g, found):
             best[g, :, :GROWS] = found
             for to in range(GRP):
-                device = at(to % 4, to // 4, lax.rem(z + gray(g), 4), core)
+                device = at(to % 4, to // 4, lax.rem(z + (0, 1, 3, 2)[g], 4), core)
 
                 def one(device=device):
                     pltpu.make_async_remote_copy(

time: 36.3 us -> 35.7 us (0.983)
  Pallas kernels: 35 us -> 34.3 us
    pallas_call x1, Pallas kernels: 35 us -> 34.3 us  [shards(): pl.pallas_call(kernel, out_shape=jax.ShapeDtypeStruct((1, ROWS), F32), in...]
where the time goes in v5:
time: 35.7 us; the launch traced here: 35.6 us
  Pallas kernels  34.3 us (96%)
  local copies, waits for them, and re-layouts  1.22 us (3%)
    pallas_call x1, Pallas kernels, shards(): pl.pallas_call(kernel, out_shape=jax.ShapeDtypeStruct((1, ROWS), F32), in...  34.3 us
    unnamed x3, local copies, waits for them, and re-layouts  1.22 us

profile of v5, /device:TPU:1, one launch (start us, length us, event | category | flops | bytes accessed | tf_op | source)
XLA Modules:
  0.0 35.6 jit_solution(17932273493568680280)
XLA Ops:
  0.0 34.3 %shard_map.28 = f32[1,192]{1,0:T(1,128)} custom-call(bf16[192,1024]{1,0:T(8,128)(2,1)} %emb_hbm.1, s32[1,192]{1,0:T(1,128)} %bitcast.3), custom_call_target="tpu_custom_call" | custom-call | tf_op jit(solution)/shard_map/pallas_call | solution.py:351
  34.3 0.0 copy-start
  34.4 0.7 %copy-done = f32[1,192]{1,0:T(1,128)S(1)} copy-done((f32[1,192]{1,0:T(1,128)S(1)}, f32[1,192]{1,0:T(1,128)}, u32[]{:S(2)}) %copy-start) | copy-done | bytes 792
  35.0 0.6 %copy.4 = f32[192]{0:T(256)} copy(f32[192]{0:T(256)S(1)} %bitcast.2) | data formatting | bytes 1536
Async XLA Ops:
  34.3 0.7 %copy-start = (f32[1,192]{1,0:T(1,128)S(1)}, f32[1,192]{1,0:T(1,128)}, u32[]{:S(2)}) copy-start(f32[1,192]{1,0:T(1,128)} %shard_map.28) | copy-start | bytes 2308

commit v6 on v5

--- a/solution.py
+++ b/solution.py
@@ -306,12 +306,12 @@
         second = jnp.maximum(second, top(theirs, 1, 0, HALF))
         first = jnp.maximum(first, top(rows, 0, HALF, 0))
         arrived(1)
+        second = jnp.maximum(jnp.maximum(second, top(theirs, 1, HALF, HALF)), -1.0)
+        give_back(3, second[:, GROWS:])
+        give_back(2, second[:, :GROWS])
         first = jnp.maximum(jnp.maximum(first, top(theirs, 1, HALF, 0)), -1.0)
+        give_back(1, first[:, GROWS:])
         give_back(0, first[:, :GROWS])
-        give_back(1, first[:, GROWS:])
-        second = jnp.maximum(jnp.maximum(second, top(theirs, 1, HALF, HALF)), -1.0)
-        give_back(2, second[:, :GROWS])
-        give_back(3, second[:, GROWS:])
 
     pltpu.make_async_copy(back, back, back_sem).wait()
     got = back[...].reshape(OWNERS, RETW)

time: 35.7 us -> 34.8 us (0.975)
  Pallas kernels: 34.3 us -> 33.5 us
    pallas_call x1, Pallas kernels: 34.3 us -> 33.5 us  [shards(): pl.pallas_call(kernel, out_shape=jax.ShapeDtypeStruct((1, ROWS), F32), in...]
where the time goes in v6:
time: 34.8 us; the launch traced here: 34.7 us
  Pallas kernels  33.5 us (96%)
  local copies, waits for them, and re-layouts  1.22 us (4%)
    pallas_call x1, Pallas kernels, shards(): pl.pallas_call(kernel, out_shape=jax.ShapeDtypeStruct((1, ROWS), F32), in...  33.5 us
    unnamed x3, local copies, waits for them, and re-layouts  1.22 us

profile of v6, /device:TPU:1, one launch (start us, length us, event | category | flops | bytes accessed | tf_op | source)
XLA Modules:
  0.0 34.7 jit_solution(16154136894487056529)
XLA Ops:
  0.0 33.5 %shard_map.28 = f32[1,192]{1,0:T(1,128)} custom-call(bf16[192,1024]{1,0:T(8,128)(2,1)} %emb_hbm.1, s32[1,192]{1,0:T(1,128)} %bitcast.3), custom_call_target="tpu_custom_call" | custom-call | tf_op jit(solution)/shard_map/pallas_call | solution.py:351
  33.5 0.0 copy-start
  33.5 0.7 %copy-done = f32[1,192]{1,0:T(1,128)S(1)} copy-done((f32[1,192]{1,0:T(1,128)S(1)}, f32[1,192]{1,0:T(1,128)}, u32[]{:S(2)}) %copy-start) | copy-done | bytes 792
  34.1 0.6 %copy.4 = f32[192]{0:T(256)} copy(f32[192]{0:T(256)S(1)} %bitcast.2) | data formatting | bytes 1536
Async XLA Ops:
  33.5 0.7 %copy-start = (f32[1,192]{1,0:T(1,128)S(1)}, f32[1,192]{1,0:T(1,128)}, u32[]{:S(2)}) copy-start(f32[1,192]{1,0:T(1,128)} %shard_map.28) | copy-start | bytes 2308

commit v7 on v6

--- a/solution.py
+++ b/solution.py
@@ -319,7 +319,8 @@
     rest = got - high.astype(F32)
     mid = rest.astype(BF16)
     low = (rest - mid.astype(F32)).astype(BF16)
-    wide = dot_tn(high, onehot_b) + dot_tn(mid, onehot_b) + dot_tn(low, onehot_b)
+    parts = jnp.concatenate([low, mid, high], axis=0)
+    wide = dot_tn(parts, jnp.concatenate([onehot_b] * 3, axis=0))
     lane = seat * CAP + rank
     out_ref[...] = jnp.sum(jnp.where(iota((RETW, ROWS), 0) == lane, wide, 0.0), axis=0, keepdims=True)
 

time: 34.8 us -> 34.8 us (level)
  no operation moved by 1% of the time
where the time goes in v7:
time: 34.8 us; the launch traced here: 34.7 us
  Pallas kernels  33.5 us (96%)
  local copies, waits for them, and re-layouts  1.22 us (4%)
    pallas_call x1, Pallas kernels, shards(): pl.pallas_call(kernel, out_shape=jax.ShapeDtypeStruct((1, ROWS), F32), in...  33.5 us
    unnamed x3, local copies, waits for them, and re-layouts  1.22 us

profile of v7, /device:TPU:1, one launch (start us, length us, event | category | flops | bytes accessed | tf_op | source)
XLA Modules:
  0.0 34.7 jit_solution(15353781151668877516)
XLA Ops:
  0.0 33.5 %shard_map.28 = f32[1,192]{1,0:T(1,128)} custom-call(bf16[192,1024]{1,0:T(8,128)(2,1)} %emb_hbm.1, s32[1,192]{1,0:T(1,128)} %bitcast.3), custom_call_target="tpu_custom_call" | custom-call | tf_op jit(solution)/shard_map/pallas_call | solution.py:352
  33.5 0.0 copy-start
  33.5 0.7 %copy-done = f32[1,192]{1,0:T(1,128)S(1)} copy-done((f32[1,192]{1,0:T(1,128)S(1)}, f32[1,192]{1,0:T(1,128)}, u32[]{:S(2)}) %copy-start) | copy-done | bytes 792
  34.1 0.6 %copy.4 = f32[192]{0:T(256)} copy(f32[192]{0:T(256)S(1)} %bitcast.2) | data formatting | bytes 1536
Async XLA Ops:
  33.5 0.7 %copy-start = (f32[1,192]{1,0:T(1,128)S(1)}, f32[1,192]{1,0:T(1,128)}, u32[]{:S(2)}) copy-start(f32[1,192]{1,0:T(1,128)} %shard_map.28) | copy-start | bytes 2308
